TPU v7x, 32 devices: a whole 2x2x4 slice. The times are simulated.
32 devices in a mesh: grp: 8 (over z, x), rep: 4 (over y, core).
Axes of the slice: x: 2, y: 2, z: 4, core: 2. Of those that a mesh axis runs over, the one named last changes fastest.
Arguments:
- series: bfloat16 [256, 5632], P('grp'), may hold values from -6 to 6
- regressors: float32 [256, 24], P('grp'), may hold values from -3 to 3
- span_ids: int32 [256], replicated, may hold values from 0 to 3, never falling along the last dimension, each value on 1 to 128 neighbouring positions
- nuisance_count: int32 [1], replicated, may hold values from 12 to 24
- owner_order: int32 [8], replicated, may hold values from 0 to 7
- vectors: bfloat16 [5632, 64], P('grp'), may hold values from -0.3125 to 0.3125
Outputs:
- projected: float32 [5632, 64], P(('grp', 'rep'))
Inputs may be any that keep to these rules, and one draw needn't show every extreme that they name: `span_ids`: never falls along frames; each of the 4 spans holds 1 to 128 frames, one exactly 128. `owner_order`: blocks may name the same slab.
All inputs are finite; a program needn't handle non-finite values.
Results may differ from a plain program's by a relative error of at most 0.0095.
Values may be sent and summed in bfloat16 or wider, within the bound.
A program may use at most 64 MiB of HBM per device.

v0:
```python
import math
import jax
import jax.numpy as jnp
from jax import lax
from jax.sharding import PartitionSpec as P

BLOCKS = 8
fast_pole = 0.64
slow_pole = 0.955
corr_limit = 0.99
norm_eps = 1e-06


def spread_2(value, axis, root):
    mine = lax.axis_index(axis) == root
    return lax.psum(jnp.where(mine, value, jnp.zeros_like(value)), axis)


def fisher_map(correlation):
    clipped = jnp.clip(correlation, -corr_limit, corr_limit)
    return 0.5 * jnp.log((1.0 + clipped) / (1.0 - clipped))


def block_operators(span_ids, frames):
    offsets = jnp.arange(128)
    lag_steps = offsets[:, None] - offsets[None, :]
    lag_clip = jnp.maximum(lag_steps, 0).astype(jnp.float32)
    operators = []
    for number in range(frames // 128):
        ids_here = span_ids[number * 128 : (number + 1) * 128]
        joined = (ids_here[:, None] == ids_here[None, :]) & (lag_steps >= 0)
        if number == 0:
            linked = jnp.zeros((128,), jnp.float32)
        else:
            linked = (ids_here == span_ids[number * 128 - 1]).astype(jnp.float32)
        pole_pair = []
        for pole_value in (fast_pole, slow_pole):
            matrix = jnp.where(
                joined, (1.0 - pole_value) * jnp.exp(lag_clip * math.log(pole_value)), 0.0
            )
            carried = linked * jnp.exp((offsets + 1).astype(jnp.float32) * math.log(pole_value))
            pole_pair.append((matrix, carried))
        operators.append(pole_pair)
    return operators


def band_pass(columns_in, operators):
    col_count = columns_in.shape[1]
    states = [jnp.zeros((col_count,), jnp.float32), jnp.zeros((col_count,), jnp.float32)]
    pieces = []
    for number, pole_pair in enumerate(operators):
        segment = columns_in[number * 128 : (number + 1) * 128]
        outputs = []
        for pole_slot in range(2):
            matrix, carried = pole_pair[pole_slot]
            response = (
                jnp.dot(matrix, segment, precision=lax.Precision.HIGHEST)
                + carried[:, None] * states[pole_slot][None, :]
            )
            states[pole_slot] = response[-1]
            outputs.append(response)
        pieces.append(outputs[0] - outputs[1])
    return jnp.concatenate(pieces, axis=0)


def nuisance_basis(filtered_nuisance, nuisance_count):
    active = (jnp.arange(filtered_nuisance.shape[1]) < nuisance_count[0]).astype(jnp.float32)
    masked = filtered_nuisance * active[None, :]
    gram_matrix = jnp.dot(masked.T, masked, precision=lax.Precision.HIGHEST) + jnp.diag(
        1.0 - active
    )
    return (masked, jnp.linalg.cholesky(gram_matrix))


def scale_columns(filtered, masked, lower_factor):
    highest = lax.Precision.HIGHEST
    right_side = jnp.dot(masked.T, filtered, precision=highest)
    halfway = lax.linalg.triangular_solve(lower_factor, right_side, left_side=True, lower=True)
    coefficients = lax.linalg.triangular_solve(
        lower_factor, halfway, left_side=True, lower=True, transpose_a=True
    )
    cleaned = filtered - jnp.dot(masked, coefficients, precision=highest)
    centered = cleaned - jnp.mean(cleaned, axis=0, keepdims=True)
    spread = lax.rsqrt(jnp.mean(centered * centered, axis=0, keepdims=True) + norm_eps)
    return (centered * spread * (1.0 / math.sqrt(centered.shape[0]))).astype(jnp.bfloat16)


def fold_tile(my_cols, vec_slab, running, part_cols):
    correlation = lax.dot_general(
        my_cols, part_cols, (((0,), (0,)), ((), ())), preferred_element_type=jnp.float32
    )
    fisher = fisher_map(correlation).astype(jnp.bfloat16)
    return running + jnp.dot(fisher, vec_slab, preferred_element_type=jnp.float32)


def local(series, regressors, span_ids, nuisance_count, owner_order, vectors):
    grp_count = lax.axis_size("grp")
    rep_count = lax.axis_size("rep")
    rep_index = lax.axis_index("rep")
    frames_loc = series.shape[0]
    frames = frames_loc * grp_count
    own_cols = series.shape[1] // (grp_count * rep_count)
    operators = block_operators(span_ids, frames)
    nuisance = lax.all_gather(regressors, "grp", axis=0, tiled=True)
    masked, lower_factor = nuisance_basis(band_pass(nuisance, operators), nuisance_count)
    quarter = series.reshape(frames_loc, grp_count, rep_count, own_cols)
    quarter = lax.dynamic_slice_in_dim(quarter, rep_index, 1, 2).reshape(
        frames_loc, grp_count, own_cols
    )
    filtered = band_pass(
        lax.all_to_all(quarter, "grp", split_axis=1, concat_axis=0, tiled=True)[:, 0, :].astype(
            jnp.float32
        ),
        operators,
    )
    unit_cols = scale_columns(filtered, masked, lower_factor)
    projected = jnp.zeros((own_cols, vectors.shape[1]), jnp.float32)
    for number in range(BLOCKS):
        piece_in, vec_slab = (
            spread_2(unit_cols, "grp", owner_order[number]),
            spread_2(vectors, "grp", owner_order[number]),
        )
        projected = fold_tile(
            unit_cols, vec_slab, projected, lax.all_gather(piece_in, "rep", axis=1, tiled=True)
        )
    return projected


def solution(mesh):
    placed = (P("grp", None), P("grp", None), P(), P(), P(), P("grp", None))
    return jax.shard_map(
        local, mesh=mesh, in_specs=placed, out_specs=P(("grp", "rep"), None), check_vma=False
    )
```

profile of v0, /device:TPU:0, one launch (start us, length us, event | category | flops | bytes accessed | tf_op | source)
XLA Modules:
  0.0 231.1 jit_solution(4362847719951692597)
XLA Ops:
  6.5 2.0 reshape.62
  8.8 0.7 copy.24
  9.6 7.3 %all-to-all-start = ((bf16[32,8,176]{2,0,1:T(8,128)(2,1)}), bf16[32,8,176]{2,0,1:T(8,128)(2,1)S(1)}, u32[]{:S(2)}, u32[]{:S(2)}) async-start(bf16[32,8,176]{2,0,1:T(8,128)(2,1)} %bitcast.70), calls=%async_computation | async-start | bytes 262144 | tf_op jit(solution)/shard_map/all_to_all | solution.py:111
  16.9 0.7 copy-done.10
  18.8 0.7 compare_select_fusion
  19.5 0.7 fusion.173
  25.2 31.1 %all-gather = f32[8,32,24]{1,2,0:T(8,128)S(1)} all-gather(f32[1,32,24]{1,2,0:T(8,128)S(1)} %bitcast.78), channel_id=1, replica_groups=mesh['grp'=8,'rep'=4] {'grp'}, dimensions={0}, use_global_device_ids=true | all-gather | bytes 27648 | tf_op jit(solution)/shard_map/all_gather | solution.py:104
  58.4 2.2 cholesky.16
  60.7 0.6 compare_reduce_fusion
  61.3 0.6 fusion.93
  62.0 1.9 custom-call.8
  63.8 0.9 broadcast_select_fusion
  67.6 0.8 broadcast_select_fusion.8
  68.4 0.9 broadcast_select_fusion.9
  69.3 95.1 %all-reduce.3.cloned.1.call-done = (bf16[704,64]{0,1:T(8,128)(2,1)}, bf16[256,176]{0,1:T(8,128)(2,1)}, bf16[704,64]{0,1:T(8,128)(2,1)}, bf16[256,176]{0,1:T(8,12...) async-done(((bf16[704,64]{0,1:T(8,128)(2,1)}, ...) | async-done | bytes 1441808 | tf_op jit(solution)/shard_map/psum | solution.py:16
  164.5 6.7 %all_gather.28 = bf16[256,704]{0,1:T(8,128)(2,1)S(1)} all-gather(bf16[256,176]{0,1:T(8,128)(2,1)} %get-tuple-element.6), channel_id=1, replica_groups=mesh['grp'=8,'rep'=4] {'rep'}, dimensions={1}, use_global_device_ids=true | all-gather | bytes 450560 | tf_op jit(solution)/shard_map/all_gather | solution.py:124
  171.2 6.5 %all_gather.29 = bf16[256,704]{0,1:T(8,128)(2,1)S(1)} all-gather(bf16[256,176]{0,1:T(8,128)(2,1)S(1)} %copy-done.7), channel_id=1, replica_groups=mesh['grp'=8,'rep'=4] {'rep'}, dimensions={1}, use_global_device_ids=true | all-gather | bytes 450560 | tf_op jit(solution)/shard_map/all_gather | solution.py:124
  177.7 6.5 %all_gather.30 = bf16[256,704]{0,1:T(8,128)(2,1)S(1)} all-gather(bf16[256,176]{0,1:T(8,128)(2,1)S(1)} %copy-done.6), channel_id=1, replica_groups=mesh['grp'=8,'rep'=4] {'rep'}, dimensions={1}, use_global_device_ids=true | all-gather | bytes 450560 | tf_op jit(solution)/shard_map/all_gather | solution.py:124
  184.2 6.5 %all_gather.31 = bf16[256,704]{0,1:T(8,128)(2,1)S(1)} all-gather(bf16[256,176]{0,1:T(8,128)(2,1)S(1)} %copy-done.5), channel_id=1, replica_groups=mesh['grp'=8,'rep'=4] {'rep'}, dimensions={1}, use_global_device_ids=true | all-gather | bytes 450560 | tf_op jit(solution)/shard_map/all_gather | solution.py:124
  190.7 6.5 %all_gather.32 = bf16[256,704]{0,1:T(8,128)(2,1)S(1)} all-gather(bf16[256,176]{0,1:T(8,128)(2,1)S(1)} %copy-done.4), channel_id=1, replica_groups=mesh['grp'=8,'rep'=4] {'rep'}, dimensions={1}, use_global_device_ids=true | all-gather | bytes 450560 | tf_op jit(solution)/shard_map/all_gather | solution.py:124
  197.3 6.5 %all_gather.33 = bf16[256,704]{0,1:T(8,128)(2,1)S(1)} all-gather(bf16[256,176]{0,1:T(8,128)(2,1)S(1)} %copy-done.3), channel_id=1, replica_groups=mesh['grp'=8,'rep'=4] {'rep'}, dimensions={1}, use_global_device_ids=true | all-gather | bytes 450560 | tf_op jit(solution)/shard_map/all_gather | solution.py:124
  203.8 6.5 %all_gather.34 = bf16[256,704]{0,1:T(8,128)(2,1)S(1)} all-gather(bf16[256,176]{0,1:T(8,128)(2,1)S(1)} %copy-done.2), channel_id=1, replica_groups=mesh['grp'=8,'rep'=4] {'rep'}, dimensions={1}, use_global_device_ids=true | all-gather | bytes 450560 | tf_op jit(solution)/shard_map/all_gather | solution.py:124
  210.3 6.5 %all_gather.35 = bf16[256,704]{0,1:T(8,128)(2,1)S(1)} all-gather(bf16[256,176]{0,1:T(8,128)(2,1)S(1)} %copy-done.1), channel_id=1, replica_groups=mesh['grp'=8,'rep'=4] {'rep'}, dimensions={1}, use_global_device_ids=true | all-gather | bytes 450560 | tf_op jit(solution)/shard_map/all_gather | solution.py:124
  223.1 1.1 convolution_add_fusion.4
  (83 shorter events, 12.1 us)
Async XLA Ops:
  9.6 55.2 %all-to-all-start = ((bf16[32,8,176]{2,0,1:T(8,128)(2,1)}), bf16[32,8,176]{2,0,1:T(8,128)(2,1)S(1)}, u32[]{:S(2)}, u32[]{:S(2)}) async-start(bf16[32,8,176]{2,0,1:T(8,128)(2,1)} %bitcast.70), calls=%async_computation | async-start | bytes 262144 | tf_op jit(solution)/shard_map/all_to_all | solution.py:111
  16.8 147.6 %all-reduce.3.cloned.1.call-start = ((), (), s32[]{:S(2)}) async-start(), calls=%async_computation.1 | async-start | bytes 3014656 | tf_op jit(solution)/shard_map/psum | solution.py:16
  16.9 0.7 copy-start.10
  18.8 0.7 copy-start.8
  22.6 2.6 %copy-start.9 = (f32[32,24]{0,1:T(8,128)S(1)}, f32[32,24]{0,1:T(8,128)}, u32[]{:S(2)}) copy-start(f32[32,24]{0,1:T(8,128)} %param.7) | copy-start | bytes 9220
  58.1 5.8 %copy-start = (bf16[704,64]{0,1:T(8,128)(2,1)S(1)}, bf16[704,64]{0,1:T(8,128)(2,1)}, u32[]{:S(2)}) copy-start(bf16[704,64]{0,1:T(8,128)(2,1)} %param.11) | copy-start | bytes 270340
  164.5 6.7 %copy-start.7 = (bf16[256,176]{0,1:T(8,128)(2,1)S(1)}, bf16[256,176]{0,1:T(8,128)(2,1)}, u32[]{:S(2)}) copy-start(bf16[256,176]{0,1:T(8,128)(2,1)} %get-tuple-element.8) | copy-start | bytes 270340
  171.2 6.5 %copy-start.6 = (bf16[256,176]{0,1:T(8,128)(2,1)S(1)}, bf16[256,176]{0,1:T(8,128)(2,1)}, u32[]{:S(2)}) copy-start(bf16[256,176]{0,1:T(8,128)(2,1)} %get-tuple-element.10) | copy-start | bytes 270340
  177.7 6.5 %copy-start.5 = (bf16[256,176]{0,1:T(8,128)(2,1)S(1)}, bf16[256,176]{0,1:T(8,128)(2,1)}, u32[]{:S(2)}) copy-start(bf16[256,176]{0,1:T(8,128)(2,1)} %get-tuple-element.12) | copy-start | bytes 270340
  184.2 6.5 %copy-start.4 = (bf16[256,176]{0,1:T(8,128)(2,1)S(1)}, bf16[256,176]{0,1:T(8,128)(2,1)}, u32[]{:S(2)}) copy-start(bf16[256,176]{0,1:T(8,128)(2,1)} %get-tuple-element.14) | copy-start | bytes 270340
  190.7 6.5 %copy-start.3 = (bf16[256,176]{0,1:T(8,128)(2,1)S(1)}, bf16[256,176]{0,1:T(8,128)(2,1)}, u32[]{:S(2)}) copy-start(bf16[256,176]{0,1:T(8,128)(2,1)} %get-tuple-element.16) | copy-start | bytes 270340
  197.3 6.5 %copy-start.2 = (bf16[256,176]{0,1:T(8,128)(2,1)S(1)}, bf16[256,176]{0,1:T(8,128)(2,1)}, u32[]{:S(2)}) copy-start(bf16[256,176]{0,1:T(8,128)(2,1)} %get-tuple-element.18) | copy-start | bytes 270340
  203.8 6.5 %copy-start.1 = (bf16[256,176]{0,1:T(8,128)(2,1)S(1)}, bf16[256,176]{0,1:T(8,128)(2,1)}, u32[]{:S(2)}) copy-start(bf16[256,176]{0,1:T(8,128)(2,1)} %get-tuple-element.20) | copy-start | bytes 270340
  210.3 6.5 %copy-start.18 = (bf16[704,64]{0,1:T(8,128)(2,1)S(1)}, bf16[704,64]{0,1:T(8,128)(2,1)}, u32[]{:S(2)}) copy-start(bf16[704,64]{0,1:T(8,128)(2,1)} %get-tuple-element.5) | copy-start | bytes 270340
  216.8 0.9 copy-start.17
  217.7 0.9 copy-start.16
  218.6 0.9 copy-start.15
  219.5 0.9 copy-start.14
  220.4 0.9 copy-start.13
  221.3 0.9 copy-start.12
  222.2 0.9 copy-start.11
Sparse Core Ops, SparseCore 0:
  69.4 94.9 all-reduce.2
where the time goes:
time: 232 us; the launch traced here: 231 us
  waiting for transfers between devices  95.1 us (41%)
  blocking collectives  83.4 us (36%)
  between operations  19.4 us (8%)
  other arithmetic  8.9 us (4%)
  local copies, waits for them, and re-layouts  8.67 us (4%)
  matrix products  8.23 us (4%)
  starting transfers between devices  7.29 us (3%)
    psum x1, waiting for transfers between devices, spread_2(): return lax.psum(jnp.where(mine, value, jnp.zeros_like(value)), axis)  95.1 us
    all_gather x8, blocking collectives, local(): lax.all_gather(piece_in, 'rep', axis=1, tiled=True)  52.3 us
    all_gather x1, blocking collectives, local(): nuisance = lax.all_gather(regressors, 'grp', axis=0, tiled=True)  31.1 us
    all_to_all x1, starting transfers between devices, local(): lax.all_to_all(quarter, 'grp', split_axis=1, concat_axis=0, tiled=True)  7.25 us
    dot_general x8, matrix products, fold_tile(): jnp.dot(fisher, vec_slab, preferred_element_type=jnp.float32)  4.66 us
  transfers between devices with their start and end apart: 2, of which 1 were waited for; matrix products, arithmetic and copies ran while one was open for 4% of the time, Pallas kernels for 0%

commit v1 on v0

--- a/solution.py
+++ b/solution.py
@@ -12,8 +12,12 @@
 
 
 def spread_2(value, axis, root):
+
+    def _start_series_all(array_in, across):
+        return jax.lax.all_gather(array_in, across).sum(axis=0)
+
     mine = lax.axis_index(axis) == root
-    return lax.psum(jnp.where(mine, value, jnp.zeros_like(value)), axis)
+    return _start_series_all(jnp.where(mine, value, jnp.zeros_like(value)), axis)
 
 
 def fisher_map(correlation):

time: 232 us -> 649 us (2.80)
  blocking collectives: 83.4 us -> 601 us
  waiting for transfers between devices: 95.1 us -> 0.01 us
  between operations: 19.4 us -> 6.12 us
    all_gather x0 -> x16, blocking collectives: none -> 521 us  [_start_series_all(): return jax.lax.all_gather(array_in, across).sum(axis=0)]
    psum x1 -> x0, waiting for transfers between devices: 95.1 us -> none  [spread_2(): return lax.psum(jnp.where(mine, value, jnp.zeros_like(value)), axis)]
    reduce_sum x0 -> x16, other arithmetic: none -> 8.4 us  [_start_series_all(): return jax.lax.all_gather(array_in, across).sum(axis=0)]
  transfers between devices with their start and end apart: 2 -> 1, of which waited for: 1 -> 0; matrix products, arithmetic and copies ran while one was open for 4% -> 2% of each run, Pallas kernels for 0% -> 0%
where the time goes in v1:
time: 649 us; the launch traced here: 648 us
  blocking collectives  601 us (93%)
  other arithmetic  14.9 us (2%)
  local copies, waits for them, and re-layouts  10.5 us (2%)
  matrix products  8.22 us (1%)
  starting transfers between devices  7.38 us (1%)
    all_gather x16, blocking collectives, _start_series_all(): return jax.lax.all_gather(array_in, across).sum(axis=0)  521 us
    all_gather x8, blocking collectives, local(): lax.all_gather(piece_in, 'rep', axis=1, tiled=True)  48.6 us
    all_gather x1, blocking collectives, local(): nuisance = lax.all_gather(regressors, 'grp', axis=0, tiled=True)  31.1 us
  transfers between devices with their start and end apart: 1, of which 0 were waited for; matrix products, arithmetic and copies ran while one was open for 2% of the time, Pallas kernels for 0%

profile of v1, /device:TPU:0, one launch (start us, length us, event | category | flops | bytes accessed | tf_op | source)
XLA Modules:
  0.0 647.8 jit_solution(716471465655234668)
XLA Ops:
  3.0 7.4 %all-to-all-start = ((bf16[32,8,176]{2,0,1:T(8,128)(2,1)}), bf16[32,8,176]{2,0,1:T(8,128)(2,1)S(1)}, u32[]{:S(2)}, u32[]{:S(2)}) async-start(bf16[32,8,176]{2,0,1:T(8,128)(2,1)} %bitcast.126), calls=%async_computation | async-start | bytes 262144 | tf_op jit(solution)/shard_map/all_to_all | solution.py:115
  11.7 31.1 %all-gather.16 = f32[8,32,24]{1,2,0:T(8,128)S(1)} all-gather(f32[1,32,24]{1,2,0:T(8,128)S(1)} %bitcast.142), channel_id=1, replica_groups=mesh['grp'=8,'rep'=4] {'grp'}, dimensions={0}, use_global_device_ids=true | all-gather | bytes 27648 | tf_op jit(solution)/shard_map/all_gather | solution.py:108
  55.5 32.1 %all-gather.17 = bf16[8,704,64]{1,2,0:T(8,128)(2,1)S(1)} all-gather(bf16[1,704,64]{1,2,0:T(8,128)(2,1)S(1)} %get-tuple-element.15), channel_id=3, replica_groups=mesh['grp'=8,'rep'=4] {'grp'}, dimensions={0}, use_global_device_ids=true | all-gather | bytes 811008 | tf_op jit(solution)/shard_map/all_gather | solution.py:17
  87.6 32.6 %all-gather.18 = bf16[8,704,64]{1,2,0:T(8,128)(2,1)S(1)} all-gather(bf16[1,704,64]{1,2,0:T(8,128)(2,1)S(1)} %get-tuple-element.14), channel_id=5, replica_groups=mesh['grp'=8,'rep'=4] {'grp'}, dimensions={0}, use_global_device_ids=true | all-gather | bytes 811008 | tf_op jit(solution)/shard_map/all_gather | solution.py:17
  120.2 32.4 %all-gather.19 = bf16[8,704,64]{1,2,0:T(8,128)(2,1)S(1)} all-gather(bf16[1,704,64]{1,2,0:T(8,128)(2,1)S(1)} %get-tuple-element.13), channel_id=7, replica_groups=mesh['grp'=8,'rep'=4] {'grp'}, dimensions={0}, use_global_device_ids=true | all-gather | bytes 811008 | tf_op jit(solution)/shard_map/all_gather | solution.py:17
  152.6 31.7 %all-gather.20 = bf16[8,704,64]{1,2,0:T(8,128)(2,1)S(1)} all-gather(bf16[1,704,64]{1,2,0:T(8,128)(2,1)S(1)} %get-tuple-element.12), channel_id=9, replica_groups=mesh['grp'=8,'rep'=4] {'grp'}, dimensions={0}, use_global_device_ids=true | all-gather | bytes 811008 | tf_op jit(solution)/shard_map/all_gather | solution.py:17
  184.3 34.4 %all-gather.21 = bf16[8,704,64]{1,2,0:T(8,128)(2,1)} all-gather(bf16[1,704,64]{1,2,0:T(8,128)(2,1)S(1)} %get-tuple-element.11), channel_id=11, replica_groups=mesh['grp'=8,'rep'=4] {'grp'}, dimensions={0}, use_global_device_ids=true | all-gather | bytes 811008 | tf_op jit(solution)/shard_map/all_gather | solution.py:17
  218.7 34.3 %all-gather.22 = bf16[8,704,64]{1,2,0:T(8,128)(2,1)} all-gather(bf16[1,704,64]{1,2,0:T(8,128)(2,1)S(1)} %get-tuple-element.10), channel_id=13, replica_groups=mesh['grp'=8,'rep'=4] {'grp'}, dimensions={0}, use_global_device_ids=true | all-gather | bytes 811008 | tf_op jit(solution)/shard_map/all_gather | solution.py:17
  253.1 34.1 %all-gather.23 = bf16[8,704,64]{1,2,0:T(8,128)(2,1)} all-gather(bf16[1,704,64]{1,2,0:T(8,128)(2,1)S(1)} %get-tuple-element.16), channel_id=15, replica_groups=mesh['grp'=8,'rep'=4] {'grp'}, dimensions={0}, use_global_device_ids=true | all-gather | bytes 811008 | tf_op jit(solution)/shard_map/all_gather | solution.py:17
  287.2 34.4 %all-gather.24 = bf16[8,704,64]{1,2,0:T(8,128)(2,1)} all-gather(bf16[1,704,64]{1,2,0:T(8,128)(2,1)S(1)} %get-tuple-element.9), channel_id=17, replica_groups=mesh['grp'=8,'rep'=4] {'grp'}, dimensions={0}, use_global_device_ids=true | all-gather | bytes 811008 | tf_op jit(solution)/shard_map/all_gather | solution.py:17
  332.2 31.5 %all-gather = bf16[2048,176]{0,1:T(8,128)(2,1)S(1)} all-gather(bf16[256,176]{0,1:T(8,128)(2,1)S(1)} %get-tuple-element.25), channel_id=2, replica_groups=mesh['grp'=8,'rep'=4] {'grp'}, dimensions={0}, use_global_device_ids=true | all-gather | bytes 811008 | tf_op jit(solution)/shard_map/all_gather | solution.py:17
  364.5 6.1 all_gather.126
  370.5 31.7 %all-gather.2 = bf16[2048,176]{0,1:T(8,128)(2,1)S(1)} all-gather(bf16[256,176]{0,1:T(8,128)(2,1)S(1)} %get-tuple-element.24), channel_id=4, replica_groups=mesh['grp'=8,'rep'=4] {'grp'}, dimensions={0}, use_global_device_ids=true | all-gather | bytes 811008 | tf_op jit(solution)/shard_map/all_gather | solution.py:17
  402.9 6.1 all_gather.131
  409.0 31.9 %all-gather.4 = bf16[2048,176]{0,1:T(8,128)(2,1)S(1)} all-gather(bf16[256,176]{0,1:T(8,128)(2,1)S(1)} %get-tuple-element.23), channel_id=6, replica_groups=mesh['grp'=8,'rep'=4] {'grp'}, dimensions={0}, use_global_device_ids=true | all-gather | bytes 811008 | tf_op jit(solution)/shard_map/all_gather | solution.py:17
  441.6 6.1 all_gather.136
  447.7 32.1 %all-gather.6 = bf16[2048,176]{0,1:T(8,128)(2,1)S(1)} all-gather(bf16[256,176]{0,1:T(8,128)(2,1)S(1)} %get-tuple-element.22), channel_id=8, replica_groups=mesh['grp'=8,'rep'=4] {'grp'}, dimensions={0}, use_global_device_ids=true | all-gather | bytes 811008 | tf_op jit(solution)/shard_map/all_gather | solution.py:17
  480.5 6.1 all_gather.141
  486.6 31.9 %all-gather.8 = bf16[2048,176]{0,1:T(8,128)(2,1)S(1)} all-gather(bf16[256,176]{0,1:T(8,128)(2,1)S(1)} %get-tuple-element.21), channel_id=10, replica_groups=mesh['grp'=8,'rep'=4] {'grp'}, dimensions={0}, use_global_device_ids=true | all-gather | bytes 811008 | tf_op jit(solution)/shard_map/all_gather | solution.py:17
  519.2 6.1 all_gather.146
  525.3 31.9 %all-gather.10 = bf16[2048,176]{0,1:T(8,128)(2,1)S(1)} all-gather(bf16[256,176]{0,1:T(8,128)(2,1)S(1)} %get-tuple-element.20), channel_id=12, replica_groups=mesh['grp'=8,'rep'=4] {'grp'}, dimensions={0}, use_global_device_ids=true | all-gather | bytes 811008 | tf_op jit(solution)/shard_map/all_gather | solution.py:17
  564.0 31.9 %all-gather.12 = bf16[2048,176]{0,1:T(8,128)(2,1)S(1)} all-gather(bf16[256,176]{0,1:T(8,128)(2,1)S(1)} %get-tuple-element.19), channel_id=14, replica_groups=mesh['grp'=8,'rep'=4] {'grp'}, dimensions={0}, use_global_device_ids=true | all-gather | bytes 811008 | tf_op jit(solution)/shard_map/all_gather | solution.py:17
  602.7 31.9 %all-gather.14 = bf16[2048,176]{0,1:T(8,128)(2,1)S(1)} all-gather(bf16[256,176]{0,1:T(8,128)(2,1)S(1)} %get-tuple-element.5), channel_id=16, replica_groups=mesh['grp'=8,'rep'=4] {'grp'}, dimensions={0}, use_global_device_ids=true | all-gather | bytes 811008 | tf_op jit(solution)/shard_map/all_gather | solution.py:17
  635.3 6.2 all_gather.161
  (108 shorter events, 45.7 us)
Async XLA Ops:
  3.0 8.7 %copy-start.11 = (f32[32,24]{0,1:T(8,128)S(1)}, f32[32,24]{0,1:T(8,128)}, u32[]{:S(2)}) copy-start(f32[32,24]{0,1:T(8,128)} %param.7) | copy-start | bytes 9220
  3.0 326.1 %all-to-all-start = ((bf16[32,8,176]{2,0,1:T(8,128)(2,1)}), bf16[32,8,176]{2,0,1:T(8,128)(2,1)S(1)}, u32[]{:S(2)}, u32[]{:S(2)}) async-start(bf16[32,8,176]{2,0,1:T(8,128)(2,1)} %bitcast.126), calls=%async_computation | async-start | bytes 262144 | tf_op jit(solution)/shard_map/all_to_all | solution.py:115
  10.4 0.7 copy-start.12
  45.9 9.6 %copy-start.4 = (bf16[704,64]{0,1:T(8,128)(2,1)S(1)}, bf16[704,64]{0,1:T(8,128)(2,1)}, u32[]{:S(2)}) copy-start(bf16[704,64]{0,1:T(8,128)(2,1)} %param.11) | copy-start | bytes 270340
  49.2 0.7 copy-start.10
  325.5 1.5 copy-start
  326.3 1.5 copy-start.1
  327.0 1.2 copy-start.2
  327.8 1.2 copy-start.3
  635.3 6.2 copy-start.9
  641.5 0.9 copy-start.8
  642.4 0.9 copy-start.7
  643.3 0.9 copy-start.6
  644.2 0.9 copy-start.5
